TPU v7x, 256 devices: a whole 4x4x8 slice. The times are simulated.
256 devices in a mesh: row: 16 (over x_lo, z), col: 16 (over y, x_hi, core).
Axes of the slice: x: 4 (x_hi: 2, x_lo: 2; x = x_hi * 2 + x_lo), y: 4, z: 8, core: 2. Of those that a mesh axis runs over, the one named last changes fastest.
Arguments:
- pair_input: float32 [512, 512, 128], P('row', 'col'), may hold values from -6 to 6
- outgoing_in: bfloat16 [128, 640], replicated, may hold values from -0.5 to 0.5
- outgoing_out: bfloat16 [128, 128], replicated, may hold values from -0.5 to 0.5
- incoming_in: bfloat16 [128, 640], replicated, may hold values from -0.5 to 0.5
- incoming_out: bfloat16 [128, 128], replicated, may hold values from -0.5 to 0.5
Outputs:
- pair_output: float32 [512, 512, 128], P('row', 'col')
All inputs are finite; a program needn't handle non-finite values.
Results may differ from a plain program's by a relative error of at most 0.011.
Values may be sent and summed in bfloat16 or wider, within the bound.
A program may use at most 128 MiB of HBM per device.

v0:
```python
import jax
import jax.numpy as jnp
from jax import lax
from jax.sharding import PartitionSpec as P


def normalize(v):
    mean = jnp.mean(v, axis=-1, keepdims=True)
    cent = v - mean
    var = jnp.mean(cent * cent, axis=-1, keepdims=True)
    return cent * lax.rsqrt(var + 1e-05)


def project(pair, w_in):
    rows_here, cols_here, chans = pair.shape
    hidden = (w_in.shape[1] - chans) // 4
    normed = normalize(pair).astype(jnp.bfloat16)
    proj = jnp.dot(normed.reshape(-1, chans), w_in, preferred_element_type=jnp.float32)
    proj = proj.reshape(rows_here, cols_here, 4 * hidden + chans)
    left = (jax.nn.sigmoid(proj[..., :hidden]) * proj[..., hidden : 2 * hidden]).astype(
        jnp.bfloat16
    )
    right = (
        jax.nn.sigmoid(proj[..., 2 * hidden : 3 * hidden]) * proj[..., 3 * hidden : 4 * hidden]
    ).astype(jnp.bfloat16)
    gate = jax.nn.sigmoid(proj[..., 4 * hidden :])
    return (left, right, gate)


def finish(pair, tri, gate, w_out):
    rows_here, cols_here, hidden = tri.shape
    tnorm = normalize(tri).astype(jnp.bfloat16)
    update = jnp.dot(tnorm.reshape(-1, hidden), w_out, preferred_element_type=jnp.float32)
    return pair + gate * update.reshape(rows_here, cols_here, w_out.shape[1])


def per_device(pair_input, outgoing_in, outgoing_out, incoming_in, incoming_out):
    left, right, gate = project(pair_input, outgoing_in)
    whole_right = lax.all_gather(right, "row", axis=0, tiled=True)
    piece = whole_right
    swapped = lax.psum_scatter(
        jnp.einsum("jkc,ikc->jic", piece, left, preferred_element_type=jnp.float32),
        "col",
        scatter_dimension=0,
        tiled=True,
    )
    tri = jnp.transpose(swapped, (1, 0, 2))
    middle = finish(pair_input, tri, gate, outgoing_out)
    left, right, gate = project(middle, incoming_in)
    whole_left = lax.all_gather(left, "col", axis=1, tiled=True)
    piece = whole_left
    tri = lax.psum_scatter(
        jnp.einsum("kic,kjc->ijc", piece, right, preferred_element_type=jnp.float32).astype(
            jnp.bfloat16
        ),
        "row",
        scatter_dimension=0,
        tiled=True,
    ).astype(jnp.float32)
    return finish(middle, tri, gate, incoming_out)


def solution(mesh):
    return jax.shard_map(
        per_device,
        mesh=mesh,
        in_specs=(P("row", "col", None), P(), P(), P(), P()),
        out_specs=P("row", "col", None),
        check_vma=False,
    )
```

profile of v0, /device:TPU:8, one launch (start us, length us, event | category | flops | bytes accessed | tf_op | source)
XLA Modules:
  0.0 429.8 jit_solution(16457944631931293853)
XLA Ops:
  6.5 0.0 copy-start
  6.5 0.0 all-gather.3.cloned.1.call-start
  6.5 1.3 reduce_sum.72
  7.8 1.4 multiply_reduce_fusion.2
  9.3 0.0 copy-done
  9.3 1.6 fusion.28
  10.9 1.0 fusion.17
  11.9 0.0 all-gather.3.cloned.1.call-update
  12.0 0.0 reduce-scatter.3.cloned.1.call-start
  12.0 2.4 copy.42
  14.4 77.4 %all-gather.3.cloned.1.call-done = bf16[512,32,128]{2,1,0:T(8,128)(2,1)} async-done(((bf16[32,32,128]{2,1,0:T(8,128)(2,1)}), bf16[512,32,128]{2,1,0:T(8,128)(2,1)}) %all-gather.3.cloned.1.call-update) | async-done | bytes 4194320 | tf_op jit(solution)/shard_map/all_gather | solution.py:39
  91.8 23.0 %copy.43 = bf16[512,32,128]{1,0,2:T(8,128)(2,1)} copy(bf16[512,32,128]{2,1,0:T(8,128)(2,1)} %all-gather.3.cloned.1.call-done) | data formatting | bytes 8388608 | tf_op jit(solution)/shard_map/all_gather | solution.py:39
  114.9 14.9 %convolution_bitcast_fusion = f32[512,32,128]{0,1,2:T(8,128)} fusion(bf16[32,32,128]{1,0,2:T(8,128)(2,1)} %copy.42, bf16[512,32,128]{1,0,2:T(8,128)(2,1)} %copy.43), kind=kOutput, calls=%fused_computation.1 | convolution fusion | flops 134217728 | bytes 12845056 | tf_op jit(solution)/shard_map/jkc,ikc->jic/dot_general | solution.py:42
  129.8 11.0 %copy.44 = f32[512,32,128]{2,1,0:T(8,128)} copy(f32[512,32,128]{0,1,2:T(8,128)} %convolution_bitcast_fusion) | data formatting | bytes 16777216 | tf_op jit(solution)/shard_map/jkc,ikc->jic/transpose | solution.py:42
  140.8 0.0 copy-start.1
  140.8 0.0 reduce-scatter.3.cloned.1.call-update
  140.8 0.0 copy-start.4
  140.8 0.0 all-gather.5.cloned.1.call-start
  140.9 107.3 %reduce-scatter.3.cloned.1.call-done = f32[32,32,128]{2,1,0:T(8,128)} async-done(((f32[512,32,128]{2,1,0:T(8,128)}), f32[32,32,128]{2,1,0:T(8,128)}) %reduce-scatter.3.cloned.1.call-update) | async-done | bytes 524304 | tf_op jit(solution)/shard_map/reduce_scatter | solution.py:41
  248.2 1.2 bitcast_reduce_fusion
  249.4 0.1 copy.45
  249.5 0.1 copy.46
  249.6 1.4 multiply_reduce_fusion.1
  251.0 0.1 copy.47
  251.1 0.1 copy.48
  251.2 1.4 multiply_convert_fusion.1
  252.6 0.0 copy-done.1
  252.6 1.1 fusion.42
  253.7 0.0 copy-start.2
  253.7 0.4 multiply_reduce_fusion
  254.1 0.4 copy-done.2
  254.5 0.0 copy-done.4
  254.5 0.6 fusion.29
  255.1 1.0 fusion.6
  256.1 0.0 all-gather.5.cloned.1.call-update
  256.1 0.2 reduce-scatter.5.cloned.1.call-start
  256.3 2.7 copy.50
  259.0 56.8 %all-gather.5.cloned.1.call-done = bf16[32,512,128]{2,1,0:T(8,128)(2,1)} async-done(((bf16[32,32,128]{2,1,0:T(8,128)(2,1)}), bf16[32,512,128]{2,1,0:T(8,128)(2,1)}) %all-gather.5.cloned.1.call-update) | async-done | bytes 4194320 | tf_op jit(solution)/shard_map/all_gather | solution.py:50
  315.8 7.9 %copy.51 = bf16[32,512,128]{1,0,2:T(8,128)(2,1)} copy(bf16[32,512,128]{2,1,0:T(8,128)(2,1)} %all-gather.5.cloned.1.call-done) | data formatting | bytes 8388608 | tf_op jit(solution)/shard_map/all_gather | solution.py:50
  323.7 5.7 %convert_bitcast_fusion = bf16[512,32,128]{0,1,2:T(8,128)(2,1)} fusion(bf16[32,32,128]{0,1,2:T(8,128)(2,1)} %copy.50, bf16[32,512,128]{1,0,2:T(8,128)(2,1)} %copy.51), kind=kOutput, calls=%fused_computation | convolution fusion | flops 136314880 | bytes 8650752 | tf_op jit(solution)/shard_map/kic,kjc->ijc/dot_general | solution.py:53
  329.4 9.2 %copy.52 = bf16[512,32,128]{2,1,0:T(8,128)(2,1)} copy(bf16[512,32,128]{0,1,2:T(8,128)(2,1)} %convert_bitcast_fusion) | data formatting | bytes 8388608 | tf_op jit(solution)/shard_map/convert_element_type | solution.py:53
  338.6 0.0 copy-start.3
  338.6 0.0 copy-start.5
  338.6 0.0 reduce-scatter.5.cloned.1.call-update
  338.6 80.0 %reduce-scatter.5.cloned.1.call-done = bf16[32,32,128]{2,1,0:T(8,128)(2,1)} async-done(((bf16[512,32,128]{2,1,0:T(8,128)(2,1)}), bf16[32,32,128]{2,1,0:T(8,128)(2,1)}) %reduce-scatter.5.cloned.1.call-update) | async-done | bytes 262160 | tf_op jit(solution)/shard_map/reduce_scatter | solution.py:52
  418.6 1.2 convert_reduce_fusion
  419.7 1.3 fusion.4
  421.1 0.0 copy-done.3
  421.1 0.0 copy-done.5
  421.1 2.2 fusion.1
  (8 shorter events, 0.1 us)
Async XLA Ops:
  6.5 2.7 copy-start
  6.5 85.3 %all-gather.3.cloned.1.call-start = ((), (), s32[]{:S(2)}) async-start(), calls=%async_computation.2 | async-start | bytes 4456448 | tf_op jit(solution)/shard_map/all_gather | solution.py:39
  12.0 236.2 %reduce-scatter.3.cloned.1.call-start = ((), (), s32[]{:S(2)}) async-start(), calls=%async_computation.3 | async-start | bytes 8912896 | tf_op jit(solution)/shard_map/reduce_scatter | solution.py:41
  140.8 111.8 %copy-start.1 = (f32[32,32,128]{2,1,0:T(8,128)S(1)}, f32[32,32,128]{2,1,0:T(8,128)}, u32[]{:S(2)}) copy-start(f32[32,32,128]{2,1,0:T(8,128)} %param.5) | copy-start | bytes 1572868
  140.8 113.7 %copy-start.4 = (bf16[128,640]{1,0:T(8,128)(2,1)S(1)}, bf16[128,640]{1,0:T(8,128)(2,1)}, u32[]{:S(2)}) copy-start(bf16[128,640]{1,0:T(8,128)(2,1)} %param.8) | copy-start | bytes 491524
  140.8 175.0 %all-gather.5.cloned.1.call-start = ((), (), s32[]{:S(2)}) async-start(), calls=%async_computation.4 | async-start | bytes 4456448 | tf_op jit(solution)/shard_map/all_gather | solution.py:50
  253.7 0.8 copy-start.2
  256.1 162.4 %reduce-scatter.5.cloned.1.call-start = ((), (), s32[]{:S(2)}) async-start(), calls=%async_computation.5 | async-start | bytes 4456448 | tf_op jit(solution)/shard_map/reduce_scatter | solution.py:52
  338.6 82.5 %copy-start.3 = (f32[32,32,128]{2,1,0:T(8,128)S(1)}, f32[32,32,128]{2,1,0:T(8,128)}, u32[]{:S(2)}) copy-start(f32[32,32,128]{2,1,0:T(8,128)} %copy-done.2) | copy-start | bytes 1572868
  338.6 82.5 %copy-start.5 = (bf16[128,128]{1,0:T(8,128)(2,1)S(1)}, bf16[128,128]{1,0:T(8,128)(2,1)}, u32[]{:S(2)}) copy-start(bf16[128,128]{1,0:T(8,128)(2,1)} %param.9) | copy-start | bytes 98308
Sparse Core Ops, SparseCore 0:
  12.1 79.6 all-gather.2
  140.9 107.2 reduce-scatter.2
  256.2 59.5 all-gather.4
  338.7 79.7 reduce-scatter.4
where the time goes:
time: 431 us; the launch traced here: 430 us
  waiting for transfers between devices  322 us (75%)
  local copies, waits for them, and re-layouts  56.9 us (13%)
  matrix products  26.2 us (6%)
  between operations  13.3 us (3%)
  other arithmetic  11.6 us (3%)
    reduce_scatter x1, waiting for transfers between devices, per_device(): lax.psum_scatter(jnp.einsum('jkc,ikc->jic', piece, left, preferred_elemen...  107 us
    reduce_scatter x1, waiting for transfers between devices, per_device(): lax.psum_scatter(jnp.einsum('kic,kjc->ijc', piece, right, preferred_eleme...  80 us
    all_gather x1, waiting for transfers between devices, per_device(): whole_right = lax.all_gather(right, 'row', axis=0, tiled=True)  77.4 us
    all_gather x1, waiting for transfers between devices, per_device(): whole_left = lax.all_gather(left, 'col', axis=1, tiled=True)  56.8 us
    all_gather x1, local copies, waits for them, and re-layouts, per_device(): whole_right = lax.all_gather(right, 'row', axis=0, tiled=True)  23 us
    dot_general x1, matrix products, per_device(): jnp.einsum('jkc,ikc->jic', piece, left, preferred_element_type=jnp.float32)  14.9 us
    transpose x1, local copies, waits for them, and re-layouts, per_device(): jnp.einsum('jkc,ikc->jic', piece, left, preferred_element_type=jnp.float32)  11 us
    convert_element_type x1, local copies, waits for them, and re-layouts, per_device(): jnp.einsum('kic,kjc->ijc', piece, right, preferred_element_type=jnp.float32)  9.17 us
  transfers between devices with their start and end apart: 4, of which 4 were waited for; matrix products, arithmetic and copies ran while one was open for 1% of the time, Pallas kernels for 0%

commit v1 on v0

v1 whole, which is shorter than its diff:
```python
import functools

import jax
import jax.numpy as jnp
from jax import lax
from jax.experimental import pallas as pl
from jax.experimental.pallas import tpu as pltpu
from jax.sharding import PartitionSpec as P

MESH = pl.DeviceIdType.MESH
F32 = jnp.float32
BF16 = jnp.bfloat16
EPS = 1e-05


def sigmoid(v):
    return 0.5 * jnp.tanh(0.5 * v) + 0.5


def device(x, y, z, core):
    return (x % 2 * 8 + z, y * 4 + x // 2 * 2 + core)


def regroup(tiles):
    lane = lax.broadcasted_iota(jnp.int32, tiles[0].shape, 1)
    low = lane < 64
    even = lane // 32 % 2 == 0
    t = list(tiles)
    for a, b in ((0, 2), (1, 3)):
        t[a], t[b] = (
            jnp.where(low, t[a], pltpu.roll(t[b], 64, 1)),
            jnp.where(low, pltpu.roll(t[a], 64, 1), t[b]),
        )
    for a, b in ((0, 1), (2, 3)):
        t[a], t[b] = (
            jnp.where(even, t[a], pltpu.roll(t[b], 32, 1)),
            jnp.where(even, pltpu.roll(t[a], 96, 1), t[b]),
        )
    return t


def kernel(
    z_ref, w1_ref, u1_ref, w2_ref, u2_ref, out_ref,
    pair, normed, gate, wt, ut, stage, stage2,
    send, recv, lmat, rmat, tsend, trecv,
    send_sem, recv_sem, ex_send, ex_recv, tsend_sem, trecv_sem, plane_sem,
):
    row, col = lax.axis_index("row"), lax.axis_index("col")
    z = row % 8
    y = col // 4
    x = col // 2 % 2 * 2 + row // 8
    core = col % 2
    me = x * 32 + y * 8 + z

    barrier = pltpu.get_barrier_semaphore()

    def plane(o):
        return device((x + o // 4) % 4, (y + o % 4) % 4, z, core)

    def greet_ring(o, _):
        pl.semaphore_signal(barrier, inc=1, device_id=device(x, y, (z + o) % 8, core), device_id_type=MESH)
        return 0

    def greet_plane(o, _):
        pl.semaphore_signal(barrier, inc=1, device_id=plane(o), device_id_type=MESH)
        return 0

    def greet_again(o, _):
        pl.semaphore_signal(plane_sem, inc=1, device_id=plane(o), device_id_type=MESH)
        return 0

    lax.fori_loop(1, 8, greet_ring, 0)
    lax.fori_loop(1, 16, greet_plane, 0)
    pl.semaphore_signal(barrier, inc=1, device_id=device(x, y, z, 1 - core), device_id_type=MESH)

    for k, (w_ref, u_ref) in enumerate(((w1_ref, u1_ref), (w2_ref, u2_ref))):
        for b in range(5):
            wt[k, b] = w_ref[:, 128 * b : 128 * b + 128].astype(F32).T.astype(BF16)
        ut[k] = u_ref[...].astype(F32).T.astype(BF16)

    for a in range(8):
        rows = z_ref[:, a].reshape(128, 128)
        pair[:, 128 * a : 128 * a + 128] = rows.T

    pl.semaphore_wait(barrier, 23)
    lax.fori_loop(1, 16, greet_again, 0)

    def norm_pair():
        v = pair[...]
        cent = v - jnp.mean(v, axis=0, keepdims=True)
        var = jnp.mean(cent * cent, axis=0, keepdims=True)
        normed[...] = (cent * lax.rsqrt(var + EPS)).astype(BF16)

    def update(k, outgoing):
        norm_pair()
        zn = normed[...]
        if k == 0:
            pl.semaphore_wait(plane_sem, 15)

        for dx in range(4):
            xd = (x + dx) % 4
            w = wt[k, :4, pl.ds(pl.multiple_of(xd * 32, 32), 32), :].reshape(128, 128)
            p = jnp.dot(w, zn, preferred_element_type=F32)
            left = sigmoid(p[0:32]) * p[32:64]
            right = sigmoid(p[64:96]) * p[96:128]
            for a in range(8):
                stage[pl.ds(a, 32, stride=16), :] = left[:, 128 * a : 128 * a + 128]
                stage[pl.ds(8 + a, 32, stride=16), :] = right[:, 128 * a : 128 * a + 128]
            send[k, xd] = stage[...].reshape(32, 16, 128).astype(BF16)

            def push(o, _, dx=dx, xd=xd):
                yd, zd = (y + o // 8) % 4, (z + o) % 8
                pltpu.make_async_remote_copy(
                    src_ref=send.at[k, xd, yd * 8 + zd],
                    dst_ref=recv.at[k, x, y * 8 + z],
                    send_sem=send_sem.at[k, dx],
                    recv_sem=recv_sem.at[k, dx],
                    device_id=device(xd, yd, zd, core),
                    device_id_type=MESH,
                ).start()
                return 0

            if dx == 0:
                recv[k, x, y * 8 + z] = send[k, x, y * 8 + z]
            lax.fori_loop(1 if dx == 0 else 0, 32, push, 0)

        gate[...] = sigmoid(jnp.dot(wt[k, 4], zn, preferred_element_type=F32))

        exchanges = []
        for dx in range(4):
            xs = (x + 4 - dx) % 4
            part = recv.at[k, xs, pl.ds(0, 31)] if dx == 0 else recv.at[k, xs]
            pltpu.make_async_copy(part, part, recv_sem.at[k, dx]).wait()
            kc = xs // 2 * 2 + core
            for zs in range(8):
                tiles = [recv[k, xs, ys * 8 + zs].astype(F32) for ys in range(4)]
                t = regroup(tiles)
                base = zs // 2 * 32
                for h in range(2):
                    pair_l = jnp.concatenate([t[2 * h][0:8], t[2 * h + 1][0:8]], axis=0)
                    pair_r = jnp.concatenate([t[2 * h][8:16], t[2 * h + 1][8:16]], axis=0)
                    here = pl.ds(base + 16 * h, 16)
                    lmat[k, kc, xs % 2, zs % 2, here, :] = pair_l.astype(BF16)
                    rmat[k, kc, xs % 2, zs % 2, here, :] = pair_r.astype(BF16)

            def swap(ref, n):
                copy = pltpu.make_async_remote_copy(
                    src_ref=ref,
                    dst_ref=ref,
                    send_sem=ex_send.at[k, dx, n],
                    recv_sem=ex_recv.at[k, dx, n],
                    device_id=device(x, y, z, 1 - core),
                    device_id_type=MESH,
                )
                copy.start()
                exchanges.append(copy)

            swap(lmat.at[k, kc, xs % 2], 0)
            if outgoing:
                swap(rmat.at[k, kc, xs % 2, 1 - core], 1)
        for copy in exchanges:
            copy.wait()

        if outgoing:
            a = jnp.concatenate([lmat[k, kc].reshape(512, 128) for kc in range(4)], axis=1)
            b = jnp.concatenate([rmat[k, kc, :, core].reshape(256, 128) for kc in range(4)], axis=1)
            tri = lax.dot_general(a, b, (((1,), (1,)), ((), ())), preferred_element_type=F32)
        else:
            a = jnp.concatenate([lmat[k, kc].reshape(512, 128) for kc in range(4)], axis=1)
            b = jnp.concatenate([rmat[k, 2 * xh + core].reshape(512, 128) for xh in range(2)], axis=1)
            tri = lax.dot_general(a, b, (((0,), (0,)), ((), ())), preferred_element_type=F32)
        for m in range(16):
            if outgoing:
                r = m // 8 * 8 + m % 4 * 2 + m // 4 % 2
            else:
                r = m % 4 * 4 + m // 4
            for n in range(2):
                tiles = [
                    tri[32 * m + 8 * u : 32 * m + 8 * u + 8, 128 * n : 128 * n + 128]
                    for u in range(4)
                ]
                for t, tile in enumerate(regroup(tiles)):
                    tsend[k, r, 4 * n + t if outgoing else 2 * t + n] = tile.astype(BF16)

        def give(o, _):
            xd, yd, zd = (x + o // 32) % 4, (y + o // 8 % 4) % 4, (z + o) % 8
            pltpu.make_async_remote_copy(
                src_ref=tsend.at[k, xd % 2 * 8 + zd, yd * 2 + xd // 2],
                dst_ref=trecv.at[k, me],
                send_sem=tsend_sem.at[k],
                recv_sem=trecv_sem.at[k],
                device_id=device(xd, yd, zd, core),
                device_id_type=MESH,
            ).start()
            return 0

        lax.fori_loop(1, 128, give, 0)
        trecv[k, me] = tsend[k, x % 2 * 8 + z, y * 2 + x // 2]
        part = trecv.at[k, pl.ds(0, 127)]
        pltpu.make_async_copy(part, part, trecv_sem.at[k]).wait()

        v = trecv[k].astype(F32)
        cent = v - jnp.mean(v, axis=0, keepdims=True)
        var = jnp.mean(cent * cent, axis=0, keepdims=True)
        stage2[...] = (cent * lax.rsqrt(var + EPS)).reshape(1024, 128)
        tn = jnp.concatenate(
            [stage2[pl.ds(a, 128, stride=8), :].astype(BF16) for a in range(8)], axis=1
        )
        change = jnp.dot(ut[k], tn, preferred_element_type=F32)
        pair[...] = pair[...] + gate[...] * change

    update(0, True)
    update(1, False)

    for a in range(8):
        out_ref[:, a] = pair[:, 128 * a : 128 * a + 128].T.reshape(4, 32, 128)

    for k in range(2):
        for dx in range(4):
            part = send.at[k, 0, pl.ds(0, 31)] if dx == 0 else send.at[k, 0]
            pltpu.make_async_copy(part, part, send_sem.at[k, dx]).wait()
        part = trecv.at[k, pl.ds(0, 127)]
        pltpu.make_async_copy(part, part, tsend_sem.at[k]).wait()


def per_device(pair_input, outgoing_in, outgoing_out, incoming_in, incoming_out):
    vmem = pl.BlockSpec(memory_space=pltpu.VMEM)
    out = pl.pallas_call(
        kernel,
        out_shape=jax.ShapeDtypeStruct((4, 8, 32, 128), F32),
        in_specs=[vmem] * 5,
        out_specs=vmem,
        scratch_shapes=[
            pltpu.VMEM((128, 1024), F32),
            pltpu.VMEM((128, 1024), BF16),
            pltpu.VMEM((128, 1024), F32),
            pltpu.VMEM((2, 5, 128, 128), BF16),
            pltpu.VMEM((2, 128, 128), BF16),
            pltpu.VMEM((512, 128), F32),
            pltpu.VMEM((1024, 128), F32),
            pltpu.VMEM((2, 4, 32, 16, 128), BF16),
            pltpu.VMEM((2, 4, 32, 16, 128), BF16),
            pltpu.VMEM((2, 4, 2, 2, 128, 128), BF16),
            pltpu.VMEM((2, 4, 2, 2, 128, 128), BF16),
            pltpu.VMEM((2, 16, 8, 8, 128), BF16),
            pltpu.VMEM((2, 128, 8, 128), BF16),
            pltpu.SemaphoreType.DMA((2, 4)),
            pltpu.SemaphoreType.DMA((2, 4)),
            pltpu.SemaphoreType.DMA((2, 4, 2)),
            pltpu.SemaphoreType.DMA((2, 4, 2)),
            pltpu.SemaphoreType.DMA((2,)),
            pltpu.SemaphoreType.DMA((2,)),
            pltpu.SemaphoreType.REGULAR,
        ],
        compiler_params=pltpu.CompilerParams(
            collective_id=0, has_side_effects=True, vmem_limit_bytes=40 << 20
        ),
    )(pair_input.reshape(4, 8, 32, 128), outgoing_in, outgoing_out, incoming_in, incoming_out)
    return out.reshape(32, 32, 128)


def solution(mesh):
    return jax.shard_map(
        per_device,
        mesh=mesh,
        in_specs=(P("row", "col", None), P(), P(), P(), P()),
        out_specs=P("row", "col", None),
        check_vma=False,
    )
```

time: 431 us -> 78.8 us (0.18)
  the two profiles are of different devices: /device:TPU:8 before, /device:TPU:1 now
where the time goes in v1:
time: 78.8 us; the launch traced here: 78.5 us
  Pallas kernels  73.3 us (93%)
  local copies, waits for them, and re-layouts  5.18 us (7%)
    pallas_call x1, Pallas kernels, per_device(): pl.pallas_call(kernel, out_shape=jax.ShapeDtypeStruct((4, 8, 32, 128), F3...  73.3 us
    unnamed x11, local copies, waits for them, and re-layouts  5.18 us

profile of v1, /device:TPU:1, one launch (start us, length us, event | category | flops | bytes accessed | tf_op | source)
XLA Modules:
  0.0 78.5 jit_solution(5556003363060047924)
XLA Ops:
  0.0 0.0 copy-start
  0.0 1.0 %copy-done = f32[32,32,128]{2,1,0:T(8,128)S(1)} copy-done((f32[32,32,128]{2,1,0:T(8,128)S(1)}, f32[32,32,128]{2,1,0:T(8,128)}, u32[]{:S(2)}) %copy-start) | copy-done | bytes 524312
  1.0 0.0 copy-start.1
  1.0 0.9 %copy-done.1 = bf16[128,640]{1,0:T(8,128)(2,1)S(1)} copy-done((bf16[128,640]{1,0:T(8,128)(2,1)S(1)}, bf16[128,640]{1,0:T(8,128)(2,1)}, u32[]{:S(2)}) %copy-start.1) | copy-done | bytes 163864
  2.0 0.0 copy-start.2
  2.0 0.9 %copy-done.2 = bf16[128,640]{1,0:T(8,128)(2,1)S(1)} copy-done((bf16[128,640]{1,0:T(8,128)(2,1)S(1)}, bf16[128,640]{1,0:T(8,128)(2,1)}, u32[]{:S(2)}) %copy-start.2) | copy-done | bytes 163864
  2.9 0.0 copy-start.3
  2.9 0.8 copy-done.3
  3.6 0.0 copy-start.4
  3.6 0.8 copy-done.4
  4.4 73.3 %shard_map.55 = f32[4,8,32,128]{3,2,1,0:T(8,128)S(1)} custom-call(f32[4,8,32,128]{3,2,1,0:T(8,128)S(1)} %bitcast.3, bf16[128,640]{1,0:T(8,128)(2,1)S(1)} %copy-done.1, bf16[128,128]{1,0:T(8,128)(2,1)S(1)} %copy-done.3, bf16[128,640]{1,0:T(8,128)(2,1)S(1)} %copy-done.2, bf16[128,128]{1,0:T(8,128)(2,1)S(1)} %copy-done.4), custom_call_target="tpu_custom_call" | custom-call | tf_op jit(solution)/shard_map/pallas_call | solution.py:228
  77.7 0.8 %copy.7 = f32[32,32,128]{2,1,0:T(8,128)} copy(f32[32,32,128]{2,1,0:T(8,128)S(1)} %bitcast.2) | data formatting | bytes 1048576
Async XLA Ops:
  0.0 1.0 %copy-start = (f32[32,32,128]{2,1,0:T(8,128)S(1)}, f32[32,32,128]{2,1,0:T(8,128)}, u32[]{:S(2)}) copy-start(f32[32,32,128]{2,1,0:T(8,128)} %param.5) | copy-start | bytes 1572868
  1.0 0.9 %copy-start.1 = (bf16[128,640]{1,0:T(8,128)(2,1)S(1)}, bf16[128,640]{1,0:T(8,128)(2,1)}, u32[]{:S(2)}) copy-start(bf16[128,640]{1,0:T(8,128)(2,1)} %w1_ref.1) | copy-start | bytes 491524
  2.0 0.9 %copy-start.2 = (bf16[128,640]{1,0:T(8,128)(2,1)S(1)}, bf16[128,640]{1,0:T(8,128)(2,1)}, u32[]{:S(2)}) copy-start(bf16[128,640]{1,0:T(8,128)(2,1)} %w2_ref.1) | copy-start | bytes 491524
  2.9 0.8 copy-start.3
  3.6 0.8 copy-start.4

commit v2 on v1

--- a/solution.py
+++ b/solution.py
@@ -17,8 +17,8 @@
     return 0.5 * jnp.tanh(0.5 * v) + 0.5
 
 
-def device(x, y, z, core):
-    return (x % 2 * 8 + z, y * 4 + x // 2 * 2 + core)
+FAR = (2, 1, 3, 0)
+RING = (4, 3, 5, 2, 6, 1, 7, 0)
 
 
 def regroup(tiles):
@@ -40,50 +40,53 @@
 
 
 def kernel(
-    z_ref, w1_ref, u1_ref, w2_ref, u2_ref, out_ref,
-    pair, normed, gate, wt, ut, stage, stage2,
+    z_hbm, w1_hbm, u1_hbm, w2_hbm, u2_hbm, out_ref,
+    z_ref, w1_ref, u1_ref, w2_ref, u2_ref, pair, normed, gate, wt, ut, stage, stage2,
     send, recv, lmat, rmat, tsend, trecv,
-    send_sem, recv_sem, ex_send, ex_recv, tsend_sem, trecv_sem, plane_sem,
+    send_sem, recv_sem, ex_send, ex_recv, tsend_sem, trecv_sem, in_sem,
 ):
     row, col = lax.axis_index("row"), lax.axis_index("col")
-    z = row % 8
-    y = col // 4
-    x = col // 2 % 2 * 2 + row // 8
-    core = col % 2
+    z = lax.rem(row, 8)
+    y = lax.div(col, 4)
+    x = lax.rem(lax.div(col, 2), 2) * 2 + lax.div(row, 8)
+    core = lax.rem(col, 2)
     me = x * 32 + y * 8 + z
+    xs = [lax.rem(x + d, 4) for d in range(4)]
+    ys = [lax.rem(y + d, 4) for d in range(4)]
+    zs = [lax.rem(z + d, 8) for d in range(8)]
+    rows = [[lax.rem(a, 2) * 8 + b for b in zs] for a in xs]
+    cols = [[b * 4 + lax.div(a, 2) * 2 + core for b in ys] for a in xs]
+    sibling = (row, col + 1 - 2 * core)
+
+    inputs = [
+        pltpu.make_async_copy(a, b, in_sem.at[n])
+        for n, (a, b) in enumerate(
+            (
+                (z_hbm, z_ref), (w1_hbm, w1_ref), (u1_hbm, u1_ref), (w2_hbm, w2_ref), (u2_hbm, u2_ref),
+            )
+        )
+    ]
+    for copy in inputs:
+        copy.start()
 
     barrier = pltpu.get_barrier_semaphore()
-
-    def plane(o):
-        return device((x + o // 4) % 4, (y + o % 4) % 4, z, core)
-
-    def greet_ring(o, _):
-        pl.semaphore_signal(barrier, inc=1, device_id=device(x, y, (z + o) % 8, core), device_id_type=MESH)
-        return 0
-
-    def greet_plane(o, _):
-        pl.semaphore_signal(barrier, inc=1, device_id=plane(o), device_id_type=MESH)
-        return 0
-
-    def greet_again(o, _):
-        pl.semaphore_signal(plane_sem, inc=1, device_id=plane(o), device_id_type=MESH)
-        return 0
-
-    lax.fori_loop(1, 8, greet_ring, 0)
-    lax.fori_loop(1, 16, greet_plane, 0)
-    pl.semaphore_signal(barrier, inc=1, device_id=device(x, y, z, 1 - core), device_id_type=MESH)
-
+    for dx in FAR:
+        for dy in FAR:
+            for dz in RING:
+                if dx or dy or dz:
+                    to = (rows[dx][dz], cols[dx][dy])
+                    pl.semaphore_signal(barrier, inc=1, device_id=to, device_id_type=MESH)
+    pl.semaphore_signal(barrier, inc=1, device_id=sibling, device_id_type=MESH)
+
+    for copy in inputs:
+        copy.wait()
     for k, (w_ref, u_ref) in enumerate(((w1_ref, u1_ref), (w2_ref, u2_ref))):
         for b in range(5):
             wt[k, b] = w_ref[:, 128 * b : 128 * b + 128].astype(F32).T.astype(BF16)
         ut[k] = u_ref[...].astype(F32).T.astype(BF16)
 
     for a in range(8):
-        rows = z_ref[:, a].reshape(128, 128)
-        pair[:, 128 * a : 128 * a + 128] = rows.T
-
-    pl.semaphore_wait(barrier, 23)
-    lax.fori_loop(1, 16, greet_again, 0)
+        pair[:, 128 * a : 128 * a + 128] = z_ref[:, a].reshape(128, 128).T
 
     def norm_pair():
         v = pair[...]
@@ -95,10 +98,10 @@
         norm_pair()
         zn = normed[...]
         if k == 0:
-            pl.semaphore_wait(plane_sem, 15)
-
-        for dx in range(4):
-            xd = (x + dx) % 4
+            pl.semaphore_wait(barrier, 128)
+
+        for dx in FAR:
+            xd = xs[dx]
             w = wt[k, :4, pl.ds(pl.multiple_of(xd * 32, 32), 32), :].reshape(128, 128)
             p = jnp.dot(w, zn, preferred_element_type=F32)
             left = sigmoid(p[0:32]) * p[32:64]
@@ -108,40 +111,39 @@
                 stage[pl.ds(8 + a, 32, stride=16), :] = right[:, 128 * a : 128 * a + 128]
             send[k, xd] = stage[...].reshape(32, 16, 128).astype(BF16)
 
-            def push(o, _, dx=dx, xd=xd):
-                yd, zd = (y + o // 8) % 4, (z + o) % 8
-                pltpu.make_async_remote_copy(
-                    src_ref=send.at[k, xd, yd * 8 + zd],
-                    dst_ref=recv.at[k, x, y * 8 + z],
-                    send_sem=send_sem.at[k, dx],
-                    recv_sem=recv_sem.at[k, dx],
-                    device_id=device(xd, yd, zd, core),
-                    device_id_type=MESH,
-                ).start()
-                return 0
-
             if dx == 0:
                 recv[k, x, y * 8 + z] = send[k, x, y * 8 + z]
-            lax.fori_loop(1 if dx == 0 else 0, 32, push, 0)
+            for dy in FAR:
+                for dz in RING:
+                    if dx or dy or dz:
+                        pltpu.make_async_remote_copy(
+                            src_ref=send.at[k, xd, ys[dy] * 8 + zs[dz]],
+                            dst_ref=recv.at[k, x, y * 8 + z],
+                            send_sem=send_sem.at[k, dx],
+                            recv_sem=recv_sem.at[k, dx],
+                            device_id=(rows[dx][dz], cols[dx][dy]),
+                            device_id_type=MESH,
+                        ).start()
 
         gate[...] = sigmoid(jnp.dot(wt[k, 4], zn, preferred_element_type=F32))
 
         exchanges = []
-        for dx in range(4):
-            xs = (x + 4 - dx) % 4
-            part = recv.at[k, xs, pl.ds(0, 31)] if dx == 0 else recv.at[k, xs]
+        for dx in FAR:
+            xo = xs[-dx]
+            part = recv.at[k, xo, pl.ds(0, 31)] if dx == 0 else recv.at[k, xo]
             pltpu.make_async_copy(part, part, recv_sem.at[k, dx]).wait()
-            kc = xs // 2 * 2 + core
-            for zs in range(8):
-                tiles = [recv[k, xs, ys * 8 + zs].astype(F32) for ys in range(4)]
+            kc = lax.div(xo, 2) * 2 + core
+            xl = lax.rem(xo, 2)
+            for n in range(8):
+                tiles = [recv[k, xo, 8 * m + n].astype(F32) for m in range(4)]
                 t = regroup(tiles)
-                base = zs // 2 * 32
+                base = n // 2 * 32
                 for h in range(2):
                     pair_l = jnp.concatenate([t[2 * h][0:8], t[2 * h + 1][0:8]], axis=0)
                     pair_r = jnp.concatenate([t[2 * h][8:16], t[2 * h + 1][8:16]], axis=0)
                     here = pl.ds(base + 16 * h, 16)
-                    lmat[k, kc, xs % 2, zs % 2, here, :] = pair_l.astype(BF16)
-                    rmat[k, kc, xs % 2, zs % 2, here, :] = pair_r.astype(BF16)
+                    lmat[k, kc, xl, n % 2, here, :] = pair_l.astype(BF16)
+                    rmat[k, kc, xl, n % 2, here, :] = pair_r.astype(BF16)
 
             def swap(ref, n):
                 copy = pltpu.make_async_remote_copy(
@@ -149,15 +151,15 @@
                     dst_ref=ref,
                     send_sem=ex_send.at[k, dx, n],
                     recv_sem=ex_recv.at[k, dx, n],
-                    device_id=device(x, y, z, 1 - core),
+                    device_id=sibling,
                     device_id_type=MESH,
                 )
                 copy.start()
                 exchanges.append(copy)
 
-            swap(lmat.at[k, kc, xs % 2], 0)
+            swap(lmat.at[k, kc, xl], 0)
             if outgoing:
-                swap(rmat.at[k, kc, xs % 2, 1 - core], 1)
+                swap(rmat.at[k, kc, xl, 1 - core], 1)
         for copy in exchanges:
             copy.wait()
 
@@ -182,20 +184,18 @@
                 for t, tile in enumerate(regroup(tiles)):
                     tsend[k, r, 4 * n + t if outgoing else 2 * t + n] = tile.astype(BF16)
 
-        def give(o, _):
-            xd, yd, zd = (x + o // 32) % 4, (y + o // 8 % 4) % 4, (z + o) % 8
+        order = [(dx, dy, dz) for dx in FAR for dy in FAR for dz in RING if dx or dy or dz]
+        order.sort(key=lambda o: -sum(min(d, n - d) for d, n in zip(o, (4, 4, 8))))
+        for dx, dy, dz in order:
             pltpu.make_async_remote_copy(
-                src_ref=tsend.at[k, xd % 2 * 8 + zd, yd * 2 + xd // 2],
+                src_ref=tsend.at[k, rows[dx][dz], ys[dy] * 2 + lax.div(xs[dx], 2)],
                 dst_ref=trecv.at[k, me],
                 send_sem=tsend_sem.at[k],
                 recv_sem=trecv_sem.at[k],
-                device_id=device(xd, yd, zd, core),
+                device_id=(rows[dx][dz], cols[dx][dy]),
                 device_id_type=MESH,
             ).start()
-            return 0
-
-        lax.fori_loop(1, 128, give, 0)
-        trecv[k, me] = tsend[k, x % 2 * 8 + z, y * 2 + x // 2]
+        trecv[k, me] = tsend[k, row, y * 2 + lax.div(x, 2)]
         part = trecv.at[k, pl.ds(0, 127)]
         pltpu.make_async_copy(part, part, trecv_sem.at[k]).wait()
 
@@ -228,9 +228,14 @@
     out = pl.pallas_call(
         kernel,
         out_shape=jax.ShapeDtypeStruct((4, 8, 32, 128), F32),
-        in_specs=[vmem] * 5,
+        in_specs=[pl.BlockSpec(memory_space=pltpu.HBM)] * 5,
         out_specs=vmem,
         scratch_shapes=[
+            pltpu.VMEM((4, 8, 32, 128), F32),
+            pltpu.VMEM((128, 640), BF16),
+            pltpu.VMEM((128, 128), BF16),
+            pltpu.VMEM((128, 640), BF16),
+            pltpu.VMEM((128, 128), BF16),
             pltpu.VMEM((128, 1024), F32),
             pltpu.VMEM((128, 1024), BF16),
             pltpu.VMEM((128, 1024), F32),
@@ -250,7 +255,7 @@
             pltpu.SemaphoreType.DMA((2, 4, 2)),
             pltpu.SemaphoreType.DMA((2,)),
             pltpu.SemaphoreType.DMA((2,)),
-            pltpu.SemaphoreType.REGULAR,
+            pltpu.SemaphoreType.DMA((5,)),
         ],
         compiler_params=pltpu.CompilerParams(
             collective_id=0, has_side_effects=True, vmem_limit_bytes=40 << 20

time: 78.8 us -> 73.6 us (0.934)
  Pallas kernels: 73.3 us -> 68.1 us
    pallas_call x1, Pallas kernels: 73.3 us -> 68.1 us  [per_device(): pl.pallas_call(kernel, out_shape=jax.ShapeDtypeStruct((4, 8, 32, 128), F3...]
where the time goes in v2:
time: 73.6 us; the launch traced here: 73.3 us
  Pallas kernels  68.1 us (93%)
  local copies, waits for them, and re-layouts  5.18 us (7%)
    pallas_call x1, Pallas kernels, per_device(): pl.pallas_call(kernel, out_shape=jax.ShapeDtypeStruct((4, 8, 32, 128), F3...  68.1 us
    unnamed x11, local copies, waits for them, and re-layouts  5.18 us

profile of v2, /device:TPU:1, one launch (start us, length us, event | category | flops | bytes accessed | tf_op | source)
XLA Modules:
  0.0 73.3 jit_solution(10866646954135772159)
XLA Ops:
  0.0 0.0 copy-start
  0.0 1.0 %copy-done = f32[32,32,128]{2,1,0:T(8,128)S(1)} copy-done((f32[32,32,128]{2,1,0:T(8,128)S(1)}, f32[32,32,128]{2,1,0:T(8,128)}, u32[]{:S(2)}) %copy-start) | copy-done | bytes 524312
  1.0 0.0 copy-start.1
  1.0 0.9 %copy-done.1 = bf16[128,640]{1,0:T(8,128)(2,1)S(1)} copy-done((bf16[128,640]{1,0:T(8,128)(2,1)S(1)}, bf16[128,640]{1,0:T(8,128)(2,1)}, u32[]{:S(2)}) %copy-start.1) | copy-done | bytes 163864
  2.0 0.0 copy-start.2
  2.0 0.9 %copy-done.2 = bf16[128,640]{1,0:T(8,128)(2,1)S(1)} copy-done((bf16[128,640]{1,0:T(8,128)(2,1)S(1)}, bf16[128,640]{1,0:T(8,128)(2,1)}, u32[]{:S(2)}) %copy-start.2) | copy-done | bytes 163864
  2.9 0.0 copy-start.3
  2.9 0.8 %copy-done.3 = bf16[128,128]{1,0:T(8,128)(2,1)S(1)} copy-done((bf16[128,128]{1,0:T(8,128)(2,1)S(1)}, bf16[128,128]{1,0:T(8,128)(2,1)}, u32[]{:S(2)}) %copy-start.3) | copy-done | bytes 32792
  3.6 0.0 copy-start.4
  3.6 0.8 %copy-done.4 = bf16[128,128]{1,0:T(8,128)(2,1)S(1)} copy-done((bf16[128,128]{1,0:T(8,128)(2,1)S(1)}, bf16[128,128]{1,0:T(8,128)(2,1)}, u32[]{:S(2)}) %copy-start.4) | copy-done | bytes 32792
  4.4 68.1 %shard_map.55 = f32[4,8,32,128]{3,2,1,0:T(8,128)S(1)} custom-call(f32[4,8,32,128]{3,2,1,0:T(8,128)S(1)} %bitcast.3, bf16[128,640]{1,0:T(8,128)(2,1)S(1)} %copy-done.1, bf16[128,128]{1,0:T(8,128)(2,1)S(1)} %copy-done.3, bf16[128,640]{1,0:T(8,128)(2,1)S(1)} %copy-done.2, bf16[128,128]{1,0:T(8,128)(2,1)S(1)} %copy-done.4), custom_call_target="tpu_custom_call" | custom-call | tf_op jit(solution)/shard_map/pallas_call | solution.py:228
  72.5 0.8 %copy.7 = f32[32,32,128]{2,1,0:T(8,128)} copy(f32[32,32,128]{2,1,0:T(8,128)S(1)} %bitcast.2) | data formatting | bytes 1048576
Async XLA Ops:
  0.0 1.0 %copy-start = (f32[32,32,128]{2,1,0:T(8,128)S(1)}, f32[32,32,128]{2,1,0:T(8,128)}, u32[]{:S(2)}) copy-start(f32[32,32,128]{2,1,0:T(8,128)} %param.5) | copy-start | bytes 1572868
  1.0 0.9 %copy-start.1 = (bf16[128,640]{1,0:T(8,128)(2,1)S(1)}, bf16[128,640]{1,0:T(8,128)(2,1)}, u32[]{:S(2)}) copy-start(bf16[128,640]{1,0:T(8,128)(2,1)} %w1_hbm.1) | copy-start | bytes 491524
  2.0 0.9 %copy-start.2 = (bf16[128,640]{1,0:T(8,128)(2,1)S(1)}, bf16[128,640]{1,0:T(8,128)(2,1)}, u32[]{:S(2)}) copy-start(bf16[128,640]{1,0:T(8,128)(2,1)} %w2_hbm.1) | copy-start | bytes 491524
  2.9 0.8 %copy-start.3 = (bf16[128,128]{1,0:T(8,128)(2,1)S(1)}, bf16[128,128]{1,0:T(8,128)(2,1)}, u32[]{:S(2)}) copy-start(bf16[128,128]{1,0:T(8,128)(2,1)} %u1_hbm.1) | copy-start | bytes 98308
  3.6 0.8 %copy-start.4 = (bf16[128,128]{1,0:T(8,128)(2,1)S(1)}, bf16[128,128]{1,0:T(8,128)(2,1)}, u32[]{:S(2)}) copy-start(bf16[128,128]{1,0:T(8,128)(2,1)} %u2_hbm.1) | copy-start | bytes 98308

commit v3 on v2

--- a/solution.py
+++ b/solution.py
@@ -19,6 +19,9 @@
 
 FAR = (2, 1, 3, 0)
 RING = (4, 3, 5, 2, 6, 1, 7, 0)
+OFFSETS = [(dx, dy, dz) for dx in FAR for dy in FAR for dz in RING]
+HALF = [(dx, dy, d) for dx in FAR for dy in FAR for d in (2, 1, 3, 0)]
+HALF.sort(key=lambda o: -(min(o[0], 4 - o[0]) + min(o[1], 4 - o[1]) + min(2 * o[2], 8 - 2 * o[2])))
 
 
 def regroup(tiles):
@@ -42,8 +45,8 @@
 def kernel(
     z_hbm, w1_hbm, u1_hbm, w2_hbm, u2_hbm, out_ref,
     z_ref, w1_ref, u1_ref, w2_ref, u2_ref, pair, normed, gate, wt, ut, stage, stage2,
-    send, recv, lmat, rmat, tsend, trecv,
-    send_sem, recv_sem, ex_send, ex_recv, tsend_sem, trecv_sem, in_sem,
+    send, recv, lown, lsib, rown, rsib, tsend, trecv,
+    send_sem, recv_sem, ex_send, ex_recv, tsend_sem, trecv_sem, in_sem, plane_sem,
 ):
     row, col = lax.axis_index("row"), lax.axis_index("col")
     z = lax.rem(row, 8)
@@ -70,12 +73,10 @@
         copy.start()
 
     barrier = pltpu.get_barrier_semaphore()
-    for dx in FAR:
-        for dy in FAR:
-            for dz in RING:
-                if dx or dy or dz:
-                    to = (rows[dx][dz], cols[dx][dy])
-                    pl.semaphore_signal(barrier, inc=1, device_id=to, device_id_type=MESH)
+    for dx, dy, dz in OFFSETS:
+        if (dx == 0) != (dy == dz == 0):
+            to = (rows[dx][dz], cols[dx][dy])
+            pl.semaphore_signal(barrier, inc=1, device_id=to, device_id_type=MESH)
     pl.semaphore_signal(barrier, inc=1, device_id=sibling, device_id_type=MESH)
 
     for copy in inputs:
@@ -97,10 +98,9 @@
     def update(k, outgoing):
         norm_pair()
         zn = normed[...]
-        if k == 0:
-            pl.semaphore_wait(barrier, 128)
-
-        for dx in FAR:
+        turns = (0, 2, 1, 3) if k == 0 else FAR
+
+        for dx in turns:
             xd = xs[dx]
             w = wt[k, :4, pl.ds(pl.multiple_of(xd * 32, 32), 32), :].reshape(128, 128)
             p = jnp.dot(w, zn, preferred_element_type=F32)
@@ -113,6 +113,13 @@
 
             if dx == 0:
                 recv[k, x, y * 8 + z] = send[k, x, y * 8 + z]
+            if k == 0 and dx == 0:
+                pl.semaphore_wait(barrier, 35)
+                for d in range(1, 4):
+                    to = (rows[d][0], cols[d][0])
+                    pl.semaphore_signal(plane_sem, inc=1, device_id=to, device_id_type=MESH)
+            if k == 0 and dx == turns[1]:
+                pl.semaphore_wait(plane_sem, 3)
             for dy in FAR:
                 for dz in RING:
                     if dx or dy or dz:
@@ -128,12 +135,11 @@
         gate[...] = sigmoid(jnp.dot(wt[k, 4], zn, preferred_element_type=F32))
 
         exchanges = []
-        for dx in FAR:
+        for dx in turns:
             xo = xs[-dx]
             part = recv.at[k, xo, pl.ds(0, 31)] if dx == 0 else recv.at[k, xo]
             pltpu.make_async_copy(part, part, recv_sem.at[k, dx]).wait()
-            kc = lax.div(xo, 2) * 2 + core
-            xl = lax.rem(xo, 2)
+            xh, xl = lax.div(xo, 2), lax.rem(xo, 2)
             for n in range(8):
                 tiles = [recv[k, xo, 8 * m + n].astype(F32) for m in range(4)]
                 t = regroup(tiles)
@@ -142,13 +148,13 @@
                     pair_l = jnp.concatenate([t[2 * h][0:8], t[2 * h + 1][0:8]], axis=0)
                     pair_r = jnp.concatenate([t[2 * h][8:16], t[2 * h + 1][8:16]], axis=0)
                     here = pl.ds(base + 16 * h, 16)
-                    lmat[k, kc, xl, n % 2, here, :] = pair_l.astype(BF16)
-                    rmat[k, kc, xl, n % 2, here, :] = pair_r.astype(BF16)
-
-            def swap(ref, n):
+                    lown[k, xh, xl, n % 2, here, :] = pair_l.astype(BF16)
+                    rown[k, xh, xl, n % 2, here, :] = pair_r.astype(BF16)
+
+            def swap(ref, there, n):
                 copy = pltpu.make_async_remote_copy(
                     src_ref=ref,
-                    dst_ref=ref,
+                    dst_ref=there,
                     send_sem=ex_send.at[k, dx, n],
                     recv_sem=ex_recv.at[k, dx, n],
                     device_id=sibling,
@@ -157,45 +163,57 @@
                 copy.start()
                 exchanges.append(copy)
 
-            swap(lmat.at[k, kc, xl], 0)
+            swap(lown.at[k, xh, xl], lsib.at[k, xh, xl], 0)
             if outgoing:
-                swap(rmat.at[k, kc, xl, 1 - core], 1)
-        for copy in exchanges:
-            copy.wait()
-
-        if outgoing:
-            a = jnp.concatenate([lmat[k, kc].reshape(512, 128) for kc in range(4)], axis=1)
-            b = jnp.concatenate([rmat[k, kc, :, core].reshape(256, 128) for kc in range(4)], axis=1)
-            tri = lax.dot_general(a, b, (((1,), (1,)), ((), ())), preferred_element_type=F32)
-        else:
-            a = jnp.concatenate([lmat[k, kc].reshape(512, 128) for kc in range(4)], axis=1)
-            b = jnp.concatenate([rmat[k, 2 * xh + core].reshape(512, 128) for xh in range(2)], axis=1)
-            tri = lax.dot_general(a, b, (((0,), (0,)), ((), ())), preferred_element_type=F32)
-        for m in range(16):
+                swap(rown.at[k, xh, xl, 1 - core], rsib.at[k, xh, xl, 1 - core], 1)
+        for half in range(2):
+            parity = core if half == 0 else 1 - core
+            if half == (0 if outgoing else 1):
+                for copy in exchanges:
+                    copy.wait()
             if outgoing:
-                r = m // 8 * 8 + m % 4 * 2 + m // 4 % 2
+                a = [m[k, i, :, parity].reshape(256, 128) for m in (lown, lsib) for i in range(2)]
+                b = [m[k, i, :, core].reshape(256, 128) for m in (rown, rsib) for i in range(2)]
+                dims = (((1,), (1,)), ((), ()))
             else:
-                r = m % 4 * 4 + m // 4
-            for n in range(2):
-                tiles = [
-                    tri[32 * m + 8 * u : 32 * m + 8 * u + 8, 128 * n : 128 * n + 128]
-                    for u in range(4)
-                ]
-                for t, tile in enumerate(regroup(tiles)):
-                    tsend[k, r, 4 * n + t if outgoing else 2 * t + n] = tile.astype(BF16)
-
-        order = [(dx, dy, dz) for dx in FAR for dy in FAR for dz in RING if dx or dy or dz]
-        order.sort(key=lambda o: -sum(min(d, n - d) for d, n in zip(o, (4, 4, 8))))
-        for dx, dy, dz in order:
-            pltpu.make_async_remote_copy(
-                src_ref=tsend.at[k, rows[dx][dz], ys[dy] * 2 + lax.div(xs[dx], 2)],
-                dst_ref=trecv.at[k, me],
-                send_sem=tsend_sem.at[k],
-                recv_sem=trecv_sem.at[k],
-                device_id=(rows[dx][dz], cols[dx][dy]),
-                device_id_type=MESH,
-            ).start()
-        trecv[k, me] = tsend[k, row, y * 2 + lax.div(x, 2)]
+                a = [(lown, lsib)[half][k, i].reshape(512, 128) for i in range(2)]
+                b = [rown[k, i].reshape(512, 128) for i in range(2)]
+                dims = (((0,), (0,)), ((), ()))
+            a, b = jnp.concatenate(a, axis=1), jnp.concatenate(b, axis=1)
+            tri = lax.dot_general(a, b, dims, preferred_element_type=F32)
+            for m in range(8):
+                r = m if outgoing else m % 4 * 2 + m // 4
+                for n in range(2):
+                    tiles = [
+                        tri[32 * m + 8 * u : 32 * m + 8 * u + 8, 128 * n : 128 * n + 128]
+                        for u in range(4)
+                    ]
+                    for t, tile in enumerate(regroup(tiles)):
+                        tsend[k, half, r, 4 * n + t if outgoing else 2 * t + n] = tile.astype(BF16)
+
+            shift = lax.rem(z + parity, 2)
+            for dx, dy, d in HALF:
+                zd = lax.rem(z + 2 * d + shift, 8)
+                to = lax.rem(xs[dx], 2) * 8 + zd
+
+                def give(half=half, dx=dx, dy=dy, to=to):
+                    pltpu.make_async_remote_copy(
+                        src_ref=tsend.at[k, half, lax.div(to, 2), ys[dy] * 2 + lax.div(xs[dx], 2)],
+                        dst_ref=trecv.at[k, me],
+                        send_sem=tsend_sem.at[k],
+                        recv_sem=trecv_sem.at[k],
+                        device_id=(to, cols[dx][dy]),
+                        device_id_type=MESH,
+                    ).start()
+
+                if dx or dy or d:
+                    give()
+                else:
+                    pl.when(shift == 1)(give)
+
+                    @pl.when(shift == 0)
+                    def _(half=half):
+                        trecv[k, me] = tsend[k, half, lax.div(row, 2), y * 2 + lax.div(x, 2)]
         part = trecv.at[k, pl.ds(0, 127)]
         pltpu.make_async_copy(part, part, trecv_sem.at[k]).wait()
 
@@ -245,9 +263,11 @@
             pltpu.VMEM((1024, 128), F32),
             pltpu.VMEM((2, 4, 32, 16, 128), BF16),
             pltpu.VMEM((2, 4, 32, 16, 128), BF16),
-            pltpu.VMEM((2, 4, 2, 2, 128, 128), BF16),
-            pltpu.VMEM((2, 4, 2, 2, 128, 128), BF16),
-            pltpu.VMEM((2, 16, 8, 8, 128), BF16),
+            pltpu.VMEM((2, 2, 2, 2, 128, 128), BF16),
+            pltpu.VMEM((2, 2, 2, 2, 128, 128), BF16),
+            pltpu.VMEM((2, 2, 2, 2, 128, 128), BF16),
+            pltpu.VMEM((2, 2, 2, 2, 128, 128), BF16),
+            pltpu.VMEM((2, 2, 8, 8, 8, 128), BF16),
             pltpu.VMEM((2, 128, 8, 128), BF16),
             pltpu.SemaphoreType.DMA((2, 4)),
             pltpu.SemaphoreType.DMA((2, 4)),
@@ -256,11 +276,19 @@
             pltpu.SemaphoreType.DMA((2,)),
             pltpu.SemaphoreType.DMA((2,)),
             pltpu.SemaphoreType.DMA((5,)),
+            pltpu.SemaphoreType.REGULAR,
         ],
         compiler_params=pltpu.CompilerParams(
             collective_id=0, has_side_effects=True, vmem_limit_bytes=40 << 20
         ),
-    )(pair_input.reshape(4, 8, 32, 128), outgoing_in, outgoing_out, incoming_in, incoming_out)
+    )(
+        *(
+            pltpu.with_memory_space_constraint(a, pltpu.HBM)
+            for a in (
+                pair_input.reshape(4, 8, 32, 128), outgoing_in, outgoing_out, incoming_in, incoming_out,
+            )
+        )
+    )
     return out.reshape(32, 32, 128)
 
 

time: 73.6 us -> 65.5 us (0.89)
  local copies, waits for them, and re-layouts: 5.18 us -> 0.8 us
  Pallas kernels: 68.1 us -> 64.6 us
    unnamed x11 -> x1, local copies, waits for them, and re-layouts: 5.18 us -> 0.8 us
    pallas_call x1, Pallas kernels: 68.1 us -> 64.6 us  [per_device(): pl.pallas_call(kernel, out_shape=jax.ShapeDtypeStruct((4, 8, 32, 128), F3...]
where the time goes in v3:
time: 65.5 us; the launch traced here: 65.4 us
  Pallas kernels  64.6 us (99%)
  local copies, waits for them, and re-layouts  0.8 us (1%)
    pallas_call x1, Pallas kernels, per_device(): pl.pallas_call(kernel, out_shape=jax.ShapeDtypeStruct((4, 8, 32, 128), F3...  64.6 us

profile of v3, /device:TPU:1, one launch (start us, length us, event | category | flops | bytes accessed | tf_op | source)
XLA Modules:
  0.0 65.4 jit_solution(6993749876190849442)
XLA Ops:
  0.0 64.6 %shard_map.55 = f32[4,8,32,128]{3,2,1,0:T(8,128)S(1)} custom-call(f32[4,8,32,128]{3,2,1,0:T(8,128)} %bitcast.3, bf16[128,640]{1,0:T(8,128)(2,1)} %w1_hbm.1, bf16[128,128]{1,0:T(8,128)(2,1)} %u1_hbm.1, bf16[128,640]{1,0:T(8,128)(2,1)} %w2_hbm.1, bf16[128,128]{1,0:T(8,128)(2,1)} %u2_hbm.1), custom_call_target="tpu_custom_call" | custom-call | tf_op jit(solution)/shard_map/pallas_call | solution.py:246
  64.6 0.8 %copy.7 = f32[32,32,128]{2,1,0:T(8,128)} copy(f32[32,32,128]{2,1,0:T(8,128)S(1)} %bitcast.2) | data formatting | bytes 1048576

commit v4 on v3

--- a/solution.py
+++ b/solution.py
@@ -56,7 +56,8 @@
     me = x * 32 + y * 8 + z
     xs = [lax.rem(x + d, 4) for d in range(4)]
     ys = [lax.rem(y + d, 4) for d in range(4)]
-    zs = [lax.rem(z + d, 8) for d in range(8)]
+    turn = 1 - 2 * lax.rem(x + y, 2)
+    zs = [lax.rem(z + 8 + turn * d, 8) for d in range(8)]
     rows = [[lax.rem(a, 2) * 8 + b for b in zs] for a in xs]
     cols = [[b * 4 + lax.div(a, 2) * 2 + core for b in ys] for a in xs]
     sibling = (row, col + 1 - 2 * core)
@@ -120,8 +121,8 @@
                     pl.semaphore_signal(plane_sem, inc=1, device_id=to, device_id_type=MESH)
             if k == 0 and dx == turns[1]:
                 pl.semaphore_wait(plane_sem, 3)
-            for dy in FAR:
-                for dz in RING:
+            for dz in RING:
+                for dy in FAR:
                     if dx or dy or dz:
                         pltpu.make_async_remote_copy(
                             src_ref=send.at[k, xd, ys[dy] * 8 + zs[dz]],

time: 65.5 us -> 63.9 us (0.976)
  Pallas kernels: 64.6 us -> 63 us
    pallas_call x1, Pallas kernels: 64.6 us -> 63 us  [per_device(): pl.pallas_call(kernel, out_shape=jax.ShapeDtypeStruct((4, 8, 32, 128), F3...]
where the time goes in v4:
time: 63.9 us; the launch traced here: 63.8 us
  Pallas kernels  63 us (99%)
  local copies, waits for them, and re-layouts  0.8 us (1%)
    pallas_call x1, Pallas kernels, per_device(): pl.pallas_call(kernel, out_shape=jax.ShapeDtypeStruct((4, 8, 32, 128), F3...  63 us

profile of v4, /device:TPU:1, one launch (start us, length us, event | category | flops | bytes accessed | tf_op | source)
XLA Modules:
  0.0 63.8 jit_solution(6272374052334810361)
XLA Ops:
  0.0 63.0 %shard_map.55 = f32[4,8,32,128]{3,2,1,0:T(8,128)S(1)} custom-call(f32[4,8,32,128]{3,2,1,0:T(8,128)} %bitcast.3, bf16[128,640]{1,0:T(8,128)(2,1)} %w1_hbm.1, bf16[128,128]{1,0:T(8,128)(2,1)} %u1_hbm.1, bf16[128,640]{1,0:T(8,128)(2,1)} %w2_hbm.1, bf16[128,128]{1,0:T(8,128)(2,1)} %u2_hbm.1), custom_call_target="tpu_custom_call" | custom-call | tf_op jit(solution)/shard_map/pallas_call | solution.py:247
  63.0 0.8 %copy.7 = f32[32,32,128]{2,1,0:T(8,128)} copy(f32[32,32,128]{2,1,0:T(8,128)S(1)} %bitcast.2) | data formatting | bytes 1048576

commit v5 on v4

--- a/solution.py
+++ b/solution.py
@@ -21,7 +21,7 @@
 RING = (4, 3, 5, 2, 6, 1, 7, 0)
 OFFSETS = [(dx, dy, dz) for dx in FAR for dy in FAR for dz in RING]
 HALF = [(dx, dy, d) for dx in FAR for dy in FAR for d in (2, 1, 3, 0)]
-HALF.sort(key=lambda o: -(min(o[0], 4 - o[0]) + min(o[1], 4 - o[1]) + min(2 * o[2], 8 - 2 * o[2])))
+HALF.sort(key=lambda o: -(min(o[0], 4 - o[0]) + min(o[1], 4 - o[1]) + min(2 * o[2] + 0.5, 7.5 - 2 * o[2])))
 
 
 def regroup(tiles):
@@ -44,7 +44,7 @@
 
 def kernel(
     z_hbm, w1_hbm, u1_hbm, w2_hbm, u2_hbm, out_ref,
-    z_ref, w1_ref, u1_ref, w2_ref, u2_ref, pair, normed, gate, wt, ut, stage, stage2,
+    z_ref, w1_ref, u1_ref, w2_ref, u2_ref, pair, normed, gate, wt, ut, gate_rows, pair_rows, stage, stage2,
     send, recv, lown, lsib, rown, rsib, tsend, trecv,
     send_sem, recv_sem, ex_send, ex_recv, tsend_sem, trecv_sem, in_sem, plane_sem,
 ):
@@ -70,9 +70,6 @@
             )
         )
     ]
-    for copy in inputs:
-        copy.start()
-
     barrier = pltpu.get_barrier_semaphore()
     for dx, dy, dz in OFFSETS:
         if (dx == 0) != (dy == dz == 0):
@@ -80,6 +77,8 @@
             pl.semaphore_signal(barrier, inc=1, device_id=to, device_id_type=MESH)
     pl.semaphore_signal(barrier, inc=1, device_id=sibling, device_id_type=MESH)
 
+    for copy in inputs:
+        copy.start()
     for copy in inputs:
         copy.wait()
     for k, (w_ref, u_ref) in enumerate(((w1_ref, u1_ref), (w2_ref, u2_ref))):
@@ -134,6 +133,10 @@
                         ).start()
 
         gate[...] = sigmoid(jnp.dot(wt[k, 4], zn, preferred_element_type=F32))
+        if k == 1:
+            for a in range(8):
+                gate_rows[a] = gate[:, 128 * a : 128 * a + 128].T
+                pair_rows[a] = pair[:, 128 * a : 128 * a + 128].T
 
         exchanges = []
         for dx in turns:
@@ -167,21 +170,24 @@
             swap(lown.at[k, xh, xl], lsib.at[k, xh, xl], 0)
             if outgoing:
                 swap(rown.at[k, xh, xl, 1 - core], rsib.at[k, xh, xl, 1 - core], 1)
+        def over_own_columns(lm, rm, parity):
+            a = jnp.concatenate([lm[k, i, :, parity].reshape(256, 128) for i in range(2)], axis=1)
+            b = jnp.concatenate([rm[k, i, :, core].reshape(256, 128) for i in range(2)], axis=1)
+            return lax.dot_general(a, b, (((1,), (1,)), ((), ())), preferred_element_type=F32)
+
+        if outgoing:
+            mine = [over_own_columns(lown, rown, p) for p in (core, 1 - core)]
         for half in range(2):
             parity = core if half == 0 else 1 - core
             if half == (0 if outgoing else 1):
                 for copy in exchanges:
                     copy.wait()
             if outgoing:
-                a = [m[k, i, :, parity].reshape(256, 128) for m in (lown, lsib) for i in range(2)]
-                b = [m[k, i, :, core].reshape(256, 128) for m in (rown, rsib) for i in range(2)]
-                dims = (((1,), (1,)), ((), ()))
+                tri = mine[half] + over_own_columns(lsib, rsib, parity)
             else:
-                a = [(lown, lsib)[half][k, i].reshape(512, 128) for i in range(2)]
-                b = [rown[k, i].reshape(512, 128) for i in range(2)]
-                dims = (((0,), (0,)), ((), ()))
-            a, b = jnp.concatenate(a, axis=1), jnp.concatenate(b, axis=1)
-            tri = lax.dot_general(a, b, dims, preferred_element_type=F32)
+                a = jnp.concatenate([(lown, lsib)[half][k, i].reshape(512, 128) for i in range(2)], axis=1)
+                b = jnp.concatenate([rown[k, i].reshape(512, 128) for i in range(2)], axis=1)
+                tri = lax.dot_general(a, b, (((0,), (0,)), ((), ())), preferred_element_type=F32)
             for m in range(8):
                 r = m if outgoing else m % 4 * 2 + m // 4
                 for n in range(2):
@@ -194,7 +200,7 @@
 
             shift = lax.rem(z + parity, 2)
             for dx, dy, d in HALF:
-                zd = lax.rem(z + 2 * d + shift, 8)
+                zd = lax.rem(z + 8 + turn * (2 * d + shift), 8)
                 to = lax.rem(xs[dx], 2) * 8 + zd
 
                 def give(half=half, dx=dx, dy=dy, to=to):
@@ -222,6 +228,12 @@
         cent = v - jnp.mean(v, axis=0, keepdims=True)
         var = jnp.mean(cent * cent, axis=0, keepdims=True)
         stage2[...] = (cent * lax.rsqrt(var + EPS)).reshape(1024, 128)
+        if k == 1:
+            for a in range(8):
+                tn = stage2[pl.ds(a, 128, stride=8), :].T.astype(BF16)
+                change = jnp.dot(tn, u2_ref[...], preferred_element_type=F32)
+                out_ref[:, a] = (pair_rows[a] + gate_rows[a] * change).reshape(4, 32, 128)
+            return
         tn = jnp.concatenate(
             [stage2[pl.ds(a, 128, stride=8), :].astype(BF16) for a in range(8)], axis=1
         )
@@ -230,9 +242,6 @@
 
     update(0, True)
     update(1, False)
-
-    for a in range(8):
-        out_ref[:, a] = pair[:, 128 * a : 128 * a + 128].T.reshape(4, 32, 128)
 
     for k in range(2):
         for dx in range(4):
@@ -260,6 +269,8 @@
             pltpu.VMEM((128, 1024), F32),
             pltpu.VMEM((2, 5, 128, 128), BF16),
             pltpu.VMEM((2, 128, 128), BF16),
+            pltpu.VMEM((8, 128, 128), F32),
+            pltpu.VMEM((8, 128, 128), F32),
             pltpu.VMEM((512, 128), F32),
             pltpu.VMEM((1024, 128), F32),
             pltpu.VMEM((2, 4, 32, 16, 128), BF16),

time: 63.9 us -> 63.9 us (level)
  no operation moved by 1% of the time
where the time goes in v5:
time: 63.9 us; the launch traced here: 63.8 us
  Pallas kernels  63 us (99%)
  local copies, waits for them, and re-layouts  0.8 us (1%)
    pallas_call x1, Pallas kernels, per_device(): pl.pallas_call(kernel, out_shape=jax.ShapeDtypeStruct((4, 8, 32, 128), F3...  63 us

profile of v5, /device:TPU:1, one launch (start us, length us, event | category | flops | bytes accessed | tf_op | source)
XLA Modules:
  0.0 63.8 jit_solution(3103595370551832875)
XLA Ops:
  0.0 63.0 %shard_map.55 = f32[4,8,32,128]{3,2,1,0:T(8,128)S(1)} custom-call(f32[4,8,32,128]{3,2,1,0:T(8,128)} %bitcast.3, bf16[128,640]{1,0:T(8,128)(2,1)} %w1_hbm.1, bf16[128,128]{1,0:T(8,128)(2,1)} %u1_hbm.1, bf16[128,640]{1,0:T(8,128)(2,1)} %w2_hbm.1, bf16[128,128]{1,0:T(8,128)(2,1)} %u2_hbm.1), custom_call_target="tpu_custom_call" | custom-call | tf_op jit(solution)/shard_map/pallas_call | solution.py:256
  63.0 0.8 %copy.7 = f32[32,32,128]{2,1,0:T(8,128)} copy(f32[32,32,128]{2,1,0:T(8,128)S(1)} %bitcast.2) | data formatting | bytes 1048576
